TPU v7x, 32 devices: a whole 2x2x4 slice. The times are simulated.
32 devices in a mesh: sect: 2 (over y), node: 4 (over z), fn: 2 (over x), sub: 2 (over core).
Axes of the slice: x: 2, y: 2, z: 4, core: 2. Of those that a mesh axis runs over, the one named last changes fastest.
Arguments:
- volume_grad: bfloat16 [2048, 32, 128], P(('sect', 'node', 'fn', 'sub')), parts along dimension 0, may hold values from -0.5 to 0.5
- volume_coords: float32 [2048, 3, 128], P(('sect', 'node', 'fn', 'sub')), parts along dimension 0, may hold values from -2.1366198 to 3
- support: int32 [2048, 32], P(('sect', 'node', 'fn', 'sub')), parts along dimension 0, may hold values from 0 to 31
- control_coords: float32 [64, 3, 128], P(('sect', 'node')), parts along dimension 0, may hold values from -2.1366198 to 3
- neighbours: int32 [64, 4], P(('sect', 'node')), parts along dimension 0, may hold values from 0 to 31
- block_inverse: float32 [64, 128, 128], P(('sect', 'node')), parts along dimension 0, may hold values from -0.09375 to 0.09375
Outputs:
- control_gradient: float32 [64, 32, 128], P(('sect', 'node')), parts along dimension 0
- adjoint: float32 [64, 32, 128], P(('sect', 'node')), parts along dimension 0
There are 2 independent parts, one for each index of `sect`. A program takes and returns all parts, laid end to end along the dimension named above; each array names one. Nothing has to cross between parts.
All inputs are finite; a program needn't handle non-finite values.
Results may differ from a plain program's by a relative error of at most 0.0034.
Values may be sent and summed in bfloat16 or wider, within the bound.
A program may use at most 64 MiB of HBM per device.

v0:
```python
import jax
import jax.numpy as jnp
from jax import lax
from jax.sharding import PartitionSpec as P

SWEEPS = 2
RADIUS = 1.2


def wendland(points, centers):
    diff = points[..., :, :, None] - centers[..., :, None, :]
    dist = jnp.sqrt(jnp.sum(diff * diff, axis=-3))
    ratio = dist / RADIUS
    inside = jnp.maximum(1.0 - ratio, 0.0)
    return (inside**4 * (4.0 * ratio + 1.0)).astype(jnp.bfloat16)


def local(volume_grad, volume_coords, support, control_coords, neighbours, block_inverse):
    all_centers = lax.all_gather(control_coords, "node", axis=0, tiled=True)
    blocks = volume_grad.shape[0]
    funcs = volume_grad.shape[1]
    width = volume_grad.shape[2]
    listed = support.shape[1]
    group = 2
    count = blocks // group
    grads = volume_grad.reshape(count, group, funcs, width)
    coords = volume_coords.reshape(count, group, 3, width)
    lists = support.reshape(count, group, listed)

    def step(total, items):
        block_grads, block_coords, block_lists = items
        centers = all_centers[block_lists]
        tiles_phi = wendland(block_coords[:, None], centers)
        tiles = jnp.einsum(
            "gfi,gkij->gkfj", block_grads, tiles_phi, preferred_element_type=jnp.float32
        )
        total = total.at[block_lists.reshape(-1)].add(tiles.reshape(-1, funcs, width))
        return (total, None)

    empty = jnp.zeros((all_centers.shape[0], funcs, width), jnp.float32)
    partial_value, _ = lax.scan(step, empty, (grads, coords, lists))
    owned = lax.psum_scatter(partial_value, "node", scatter_dimension=0, tiled=True)
    control_gradient = lax.psum(owned, ("fn", "sub"))
    adjoint = jnp.einsum(
        "cfi,cij->cfj", control_gradient, block_inverse, precision=lax.Precision.HIGHEST
    )
    pair_phi = wendland(all_centers[neighbours], control_coords[:, None])
    for sweep in range(SWEEPS):
        values = lax.all_gather(adjoint.astype(jnp.bfloat16), "node", axis=0, tiled=True)
        near = values[neighbours]
        coupling = jnp.einsum("ckfi,ckij->cfj", near, pair_phi, preferred_element_type=jnp.float32)
        adjoint = jnp.einsum(
            "cfi,cij->cfj",
            control_gradient - coupling,
            block_inverse,
            precision=lax.Precision.HIGHEST,
        )
    return (control_gradient, adjoint)


def solution(mesh):
    return jax.shard_map(
        local,
        mesh=mesh,
        in_specs=(
            P(("sect", "node", "fn", "sub"), None, None),
            P(("sect", "node", "fn", "sub"), None, None),
            P(("sect", "node", "fn", "sub"), None),
            P(("sect", "node"), None, None),
            P(("sect", "node"), None),
            P(("sect", "node"), None, None),
        ),
        out_specs=(P(("sect", "node"), None, None), P(("sect", "node"), None, None)),
        check_vma=False,
    )
```

profile of v0, /device:TPU:0, one launch (start us, length us, event | category | flops | bytes accessed | tf_op | source)
XLA Modules:
  0.0 401.6 jit_solution(12092101449089686073)
XLA Ops:
  9.0 15.0 %all_gather.9 = f32[32,3,128]{2,0,1:T(8,128)S(1)} all-gather(f32[8,3,128]{2,0,1:T(8,128)} %param.11), channel_id=1, replica_groups=mesh['sect'=2,'node'=4,'fn'=2,'sub'=2] {'node'}, dimensions={0}, use_global_device_ids=true | all-gather | bytes 61440 | tf_op jit(solution)/shard_map/all_gather | solution.py:19
  24.1 280.2 %while.12 = (s32[]{:T(128)}, f32[32,32,128]{2,1,0:T(8,128)S(1)}, s32[32,2,32]{2,1,0:T(2,128)S(1)}, f32[32,2,3,128]{3,2,1,0:T(4,128)S(1)}, f32[32,3,128]{2,1,0:T(...) while((s32[]{:T(128)}, f32[32,32,128]{2,1,0:T(8,128)S(1)}, s32[32,2,32]{2,1,0:T(2,128)S(1)}, ...), condition=%wide.region_3.4_spmd, body=%wide.region_0.3_spmd.sunk | while | flops 85198208 | bytes 12910689 | solution.py:41
  38.5 3.1 scatter_fusion
  47.2 3.1 scatter_fusion
  73.5 3.1 scatter_fusion
  82.3 3.1 scatter_fusion
  108.5 3.1 scatter_fusion
  126.0 3.1 scatter_fusion
  143.6 3.1 scatter_fusion
  152.3 3.1 scatter_fusion
  178.6 3.1 scatter_fusion
  187.3 3.1 scatter_fusion
  204.8 3.1 scatter_fusion
  213.6 3.1 scatter_fusion
  222.4 3.1 scatter_fusion
  239.9 3.1 scatter_fusion
  248.6 3.1 scatter_fusion
  266.1 3.1 scatter_fusion
  274.9 3.1 scatter_fusion
  306.0 3.4 multiply_reduce_fusion.1
  309.4 18.7 %reduce-scatter.2.cloned.1.call-done = f32[8,32,128]{2,1,0:T(8,128)} async-done(((f32[32,32,128]{2,1,0:T(8,128)}), f32[8,32,128]{2,1,0:T(8,128)}) %reduce-scatter.2.cloned.1.call-update) | async-done | bytes 131088 | tf_op jit(solution)/shard_map/reduce_scatter | solution.py:42
  330.8 29.3 %all-reduce.2.cloned.1.call-done = f32[8,32,128]{2,1,0:T(8,128)} async-done(((f32[8,32,128]{2,1,0:T(8,128)}), f32[8,32,128]{2,1,0:T(8,128)}) %all-reduce.2.cloned.1.call-update) | async-done | bytes 131088 | tf_op jit(solution)/shard_map/psum | solution.py:43
  361.7 13.9 %all_gather.10 = bf16[32,32,128]{2,1,0:T(8,128)(2,1)S(1)} all-gather(bf16[8,32,128]{2,1,0:T(8,128)(2,1)S(1)} %convolution_convert_fusion.1), channel_id=1, replica_groups=mesh['sect'=2,'node'=4,'fn'=2,'sub'=2] {'node'}, dimensions={0}, use_global_device_ids=true | all-gather | bytes 327680 | tf_op jit(solution)/shard_map/all_gather | solution.py:49
  377.9 14.1 %all_gather.11 = bf16[32,32,128]{2,1,0:T(8,128)(2,1)S(1)} all-gather(bf16[8,32,128]{2,1,0:T(8,128)(2,1)S(1)} %convolution_convert_fusion), channel_id=1, replica_groups=mesh['sect'=2,'node'=4,'fn'=2,'sub'=2] {'node'}, dimensions={0}, use_global_device_ids=true | all-gather | bytes 327680 | tf_op jit(solution)/shard_map/all_gather | solution.py:49
  (336 shorter events, 238.3 us)
Async XLA Ops:
  7.2 353.0 %copy-start = (f32[8,128,128]{2,1,0:T(8,128)S(1)}, f32[8,128,128]{2,1,0:T(8,128)}, u32[]{:S(2)}) copy-start(f32[8,128,128]{2,1,0:T(8,128)} %param.13) | copy-start | bytes 1572868
  7.2 321.0 %reduce-scatter.2.cloned.1.call-start = ((), (), s32[]{:S(2)}) async-start(), calls=%async_computation.1 | async-start | bytes 655360 | tf_op jit(solution)/shard_map/reduce_scatter | solution.py:42
  24.1 281.1 %copy-start.3 = (f32[8,3,128]{2,0,1:T(8,128)S(1)}, f32[8,3,128]{2,0,1:T(8,128)}, u32[]{:S(2)}) copy-start(f32[8,3,128]{2,0,1:T(8,128)} %param.11) | copy-start | bytes 36868
  24.1 281.1 %copy-start.4 = (s32[8,4]{0,1:T(4,128)S(1)}, s32[8,4]{0,1:T(4,128)}, u32[]{:S(2)}) copy-start(s32[8,4]{0,1:T(4,128)} %param.12) | copy-start | bytes 388
  304.3 0.8 copy-start.1
  305.1 55.0 %all-reduce.2.cloned.1.call-start = ((), (), s32[]{:S(2)}) async-start(), calls=%async_computation.2 | async-start | bytes 262144 | tf_op jit(solution)/shard_map/psum | solution.py:43
  360.1 32.5 %copy-start.2 = (f32[8,32,128]{2,1,0:T(8,128)S(1)}, f32[8,32,128]{2,1,0:T(8,128)}, u32[]{:S(2)}) copy-start(f32[8,32,128]{2,1,0:T(8,128)} %all-reduce.2.cloned.1.call-done) | copy-start | bytes 393220
Sparse Core Ops, SparseCore 0:
  305.3 22.8 reduce-scatter.1
  330.5 29.6 all-reduce.1
where the time goes:
time: 405 us; the launch traced here: 402 us
  other arithmetic  161 us (40%)
  matrix products  102 us (25%)
  waiting for transfers between devices  48 us (12%)
  blocking collectives  42.9 us (11%)
  local copies, waits for them, and re-layouts  31.8 us (8%)
  between operations  14.2 us (4%)
    scatter-add x32, other arithmetic, step(): total.at[block_lists.reshape(-1)].add(tiles.reshape(-1, funcs, width))  100 us
    dot_general x32, matrix products, step(): jnp.einsum('gfi,gkij->gkfj', block_grads, tiles_phi, preferred_element_ty...  97 us
    reduce_sum x33, other arithmetic, wendland(): dist = jnp.sqrt(jnp.sum(diff * diff, axis=-3))  57.5 us
    psum x1, waiting for transfers between devices, local(): control_gradient = lax.psum(owned, ('fn', 'sub'))  29.3 us
    all_gather x2, blocking collectives, local(): lax.all_gather(adjoint.astype(jnp.bfloat16), 'node', axis=0, tiled=True)  28 us
    gather x32, local copies, waits for them, and re-layouts, step(): centers = all_centers[block_lists]  21 us
    reduce_scatter x1, waiting for transfers between devices, local(): lax.psum_scatter(partial_value, 'node', scatter_dimension=0, tiled=True)  18.7 us
    all_gather x1, blocking collectives, local(): all_centers = lax.all_gather(control_coords, 'node', axis=0, tiled=True)  15 us
  transfers between devices with their start and end apart: 2, of which 2 were waited for; matrix products, arithmetic and copies ran while one was open for 2% of the time, Pallas kernels for 0%

commit v1 on v0

--- a/solution.py
+++ b/solution.py
@@ -40,7 +40,8 @@
     empty = jnp.zeros((all_centers.shape[0], funcs, width), jnp.float32)
     partial_value, _ = lax.scan(step, empty, (grads, coords, lists))
     owned = lax.psum_scatter(partial_value, "node", scatter_dimension=0, tiled=True)
-    control_gradient = lax.psum(owned, ("fn", "sub"))
+    touch_ranges_on_mesh = lambda raw, bus_axis: jnp.sum(jax.lax.all_gather(raw, bus_axis), 0)
+    control_gradient = touch_ranges_on_mesh(owned, ("fn", "sub"))
     adjoint = jnp.einsum(
         "cfi,cij->cfj", control_gradient, block_inverse, precision=lax.Precision.HIGHEST
     )

time: 405 us -> 378 us (0.933)
  waiting for transfers between devices: 48 us -> 19 us
  blocking collectives: 42.9 us -> 50.6 us
    psum x1 -> x0, waiting for transfers between devices: 29.3 us -> none  [local(): control_gradient = lax.psum(owned, ('fn', 'sub'))]
    all_gather x0 -> x1, blocking collectives: none -> 7.24 us  [local(): jax.lax.all_gather(raw, bus_axis)]
  transfers between devices with their start and end apart: 2 -> 1, of which waited for: 2 -> 1; matrix products, arithmetic and copies ran while one was open for 2% -> 1% of each run, Pallas kernels for 0% -> 0%
where the time goes in v1:
time: 378 us; the launch traced here: 375 us
  other arithmetic  158 us (42%)
  matrix products  99.9 us (26%)
  blocking collectives  50.6 us (13%)
  local copies, waits for them, and re-layouts  31.2 us (8%)
  waiting for transfers between devices  19 us (5%)
  between operations  14.2 us (4%)
    scatter-add x32, other arithmetic, step(): total.at[block_lists.reshape(-1)].add(tiles.reshape(-1, funcs, width))  100 us
    dot_general x32, matrix products, step(): jnp.einsum('gfi,gkij->gkfj', block_grads, tiles_phi, preferred_element_ty...  97 us
    reduce_sum x33, other arithmetic, wendland(): dist = jnp.sqrt(jnp.sum(diff * diff, axis=-3))  56.2 us
    all_gather x2, blocking collectives, local(): lax.all_gather(adjoint.astype(jnp.bfloat16), 'node', axis=0, tiled=True)  28.4 us
    gather x32, local copies, waits for them, and re-layouts, step(): centers = all_centers[block_lists]  21 us
    reduce_scatter x1, waiting for transfers between devices, local(): lax.psum_scatter(partial_value, 'node', scatter_dimension=0, tiled=True)  19 us
    all_gather x1, blocking collectives, local(): all_centers = lax.all_gather(control_coords, 'node', axis=0, tiled=True)  15 us
  transfers between devices with their start and end apart: 1, of which 1 were waited for; matrix products, arithmetic and copies ran while one was open for 1% of the time, Pallas kernels for 0%

profile of v1, /device:TPU:0, one launch (start us, length us, event | category | flops | bytes accessed | tf_op | source)
XLA Modules:
  0.0 374.8 jit_solution(16474226288439371210)
XLA Ops:
  9.0 15.0 %all_gather.15 = f32[32,3,128]{2,0,1:T(8,128)S(1)} all-gather(f32[8,3,128]{2,0,1:T(8,128)} %param.11), channel_id=1, replica_groups=mesh['sect'=2,'node'=4,'fn'=2,'sub'=2] {'node'}, dimensions={0}, use_global_device_ids=true | all-gather | bytes 61440 | tf_op jit(solution)/shard_map/all_gather | solution.py:19
  24.1 280.2 %while.12 = (s32[]{:T(128)}, f32[32,32,128]{2,1,0:T(8,128)S(1)}, s32[32,2,32]{2,1,0:T(2,128)S(1)}, f32[32,2,3,128]{3,2,1,0:T(4,128)S(1)}, f32[32,3,128]{2,1,0:T(...) while((s32[]{:T(128)}, f32[32,32,128]{2,1,0:T(8,128)S(1)}, s32[32,2,32]{2,1,0:T(2,128)S(1)}, ...), condition=%wide.region_3.4_spmd, body=%wide.region_0.3_spmd.sunk | while | flops 85198208 | bytes 12910689 | solution.py:41
  38.5 3.1 scatter_fusion
  47.2 3.1 scatter_fusion
  73.5 3.1 scatter_fusion
  82.3 3.1 scatter_fusion
  108.5 3.1 scatter_fusion
  126.0 3.1 scatter_fusion
  143.6 3.1 scatter_fusion
  152.3 3.1 scatter_fusion
  178.6 3.1 scatter_fusion
  187.3 3.1 scatter_fusion
  204.8 3.1 scatter_fusion
  213.6 3.1 scatter_fusion
  222.4 3.1 scatter_fusion
  239.9 3.1 scatter_fusion
  248.6 3.1 scatter_fusion
  266.1 3.1 scatter_fusion
  274.9 3.1 scatter_fusion
  292.4 3.1 scatter_fusion
  309.1 19.0 %reduce-scatter.2.cloned.1.call-done = f32[8,32,128]{2,1,0:T(8,128)} async-done(((f32[32,32,128]{2,1,0:T(8,128)}), f32[8,32,128]{2,1,0:T(8,128)}) %reduce-scatter.2.cloned.1.call-update) | async-done | bytes 131088 | tf_op jit(solution)/shard_map/reduce_scatter | solution.py:42
  328.1 7.2 %all-gather = f32[32,32,128]{2,1,0:T(8,128)S(1)} all-gather(f32[8,32,128]{2,1,0:T(8,128)} %reduce-scatter.2.cloned.1.call-done), channel_id=2, replica_groups=mesh['sect'=2,'node'=4,'fn'=2,'sub'=2] {'fn','sub'}, dimensions={0}, use_global_device_ids=true | all-gather | bytes 655360 | tf_op jit(solution)/shard_map/all_gather | solution.py:43
  336.0 14.5 %all_gather.18 = bf16[32,32,128]{2,1,0:T(8,128)(2,1)S(1)} all-gather(bf16[8,32,128]{2,1,0:T(8,128)(2,1)S(1)} %convolution_convert_fusion.1), channel_id=1, replica_groups=mesh['sect'=2,'node'=4,'fn'=2,'sub'=2] {'node'}, dimensions={0}, use_global_device_ids=true | all-gather | bytes 327680 | tf_op jit(solution)/shard_map/all_gather | solution.py:50
  351.9 13.9 %all_gather.19 = bf16[32,32,128]{2,1,0:T(8,128)(2,1)S(1)} all-gather(bf16[8,32,128]{2,1,0:T(8,128)(2,1)S(1)} %convolution_convert_fusion), channel_id=1, replica_groups=mesh['sect'=2,'node'=4,'fn'=2,'sub'=2] {'node'}, dimensions={0}, use_global_device_ids=true | all-gather | bytes 327680 | tf_op jit(solution)/shard_map/all_gather | solution.py:50
  (334 shorter events, 233.1 us)
Async XLA Ops:
  7.2 328.3 %copy-start = (f32[8,128,128]{2,1,0:T(8,128)S(1)}, f32[8,128,128]{2,1,0:T(8,128)}, u32[]{:S(2)}) copy-start(f32[8,128,128]{2,1,0:T(8,128)} %param.13) | copy-start | bytes 1572868
  7.2 321.0 %reduce-scatter.2.cloned.1.call-start = ((), (), s32[]{:S(2)}) async-start(), calls=%async_computation.1 | async-start | bytes 655360 | tf_op jit(solution)/shard_map/reduce_scatter | solution.py:42
  24.1 281.0 %copy-start.3 = (f32[8,3,128]{2,0,1:T(8,128)S(1)}, f32[8,3,128]{2,0,1:T(8,128)}, u32[]{:S(2)}) copy-start(f32[8,3,128]{2,0,1:T(8,128)} %param.11) | copy-start | bytes 36868
  24.1 281.0 %copy-start.4 = (s32[8,4]{0,1:T(4,128)S(1)}, s32[8,4]{0,1:T(4,128)}, u32[]{:S(2)}) copy-start(s32[8,4]{0,1:T(4,128)} %param.12) | copy-start | bytes 388
  304.3 0.8 copy-start.1
  335.4 32.5 %copy-start.2 = (f32[8,32,128]{2,1,0:T(8,128)}, f32[8,32,128]{2,1,0:T(8,128)S(1)}, u32[]{:S(2)}) copy-start(f32[8,32,128]{2,1,0:T(8,128)S(1)} %reduce_sum.30) | copy-start | bytes 393220
Sparse Core Ops, SparseCore 0:
  305.2 22.8 reduce-scatter.1
